TPU v7x, 512 devices: a whole 4x8x8 slice. The times are simulated.
512 devices in a mesh: seq: 16 (over z_hi, y), kvh: 8 (over x, core), ans: 4 (over z_lo).
Axes of the slice: x: 4, y: 8, z: 8 (z_hi: 2, z_lo: 4; z = z_hi * 4 + z_lo), core: 2. Of those that a mesh axis runs over, the one named last changes fastest.
Arguments:
- query_pre: bfloat16 [2048, 8192], P('seq', ('kvh', 'ans')), may hold values from -128 to 128
- key_pre: bfloat16 [2048, 1024], P('seq', 'kvh'), may hold values from -128 to 128
- value_pre: bfloat16 [2048, 1024], P('seq', 'kvh'), may hold values from -6 to 6
- grad_pre: bfloat16 [2048, 8192], P('seq', ('kvh', 'ans')), may hold values from -6 to 6
- query_ans: bfloat16 [16, 512, 8192], P('seq', 'ans', 'kvh'), may hold values from -128 to 128
- key_ans: bfloat16 [16, 512, 1024], P('seq', 'ans', 'kvh'), may hold values from -6 to 6
- value_ans: bfloat16 [16, 512, 1024], P('seq', 'ans', 'kvh'), may hold values from -6 to 6
- grad_ans: bfloat16 [16, 512, 8192], P('seq', 'ans', 'kvh'), may hold values from -6 to 6
- lengths: int32 [16], replicated, may hold values from 1 to 512, 5120 in all
Outputs:
- prefix_out: bfloat16 [2048, 8192], P('seq', ('kvh', 'ans'))
- prefix_qgrad: bfloat16 [2048, 8192], P('seq', ('kvh', 'ans'))
- prefix_kgrad: bfloat16 [2048, 1024], P('seq', 'kvh')
- prefix_vgrad: bfloat16 [2048, 1024], P('seq', 'kvh')
- answer_out: bfloat16 [16, 512, 8192], P('seq', 'ans', 'kvh')
- answer_qgrad: bfloat16 [16, 512, 8192], P('seq', 'ans', 'kvh')
- answer_kgrad: bfloat16 [16, 512, 1024], P('seq', 'ans', 'kvh')
- answer_vgrad: bfloat16 [16, 512, 1024], P('seq', 'ans', 'kvh')
Inputs may be any that keep to these rules, and one draw needn't show every extreme that they name: Answer a's first lengths[a] positions are real, the rest padding; in every draw some answer fills all 512 positions.
All inputs are finite; a program needn't handle non-finite values.
Results may differ from a plain program's by a relative error of at most 0.0095.
Values may be sent and summed in bfloat16 or wider, within the bound.
A program may use at most 64 MiB of HBM per device.

v0:
```python
import math

import jax
import jax.numpy as jnp
from jax import lax
from jax.sharding import PartitionSpec as P

DH = 128
QH = 64
KVH = 8


def attend(queries, key_rows, value_rows, out_grads, positions, open_cols):
    total_rows, width = queries.shape
    block = math.gcd(total_rows, 512)
    count = total_rows // block
    factor = 1.0 / math.sqrt(width)
    columns = jnp.arange(key_rows.shape[0], dtype=jnp.int32)

    def block_step(totals, pieces):
        grad_keys, grad_values = totals
        q_block, g_block, pos_block = pieces
        scores = jnp.dot(q_block, key_rows.T, preferred_element_type=jnp.float32) * factor
        visible = (columns[None, :] < open_cols) | (
            columns[None, :] - open_cols <= pos_block[:, None]
        )
        scores = jnp.where(visible, scores, -jnp.inf)
        weights = jax.nn.softmax(scores, axis=-1)
        weights_low = weights.astype(jnp.bfloat16)
        result = jnp.dot(weights_low, value_rows, preferred_element_type=jnp.float32)
        dweights = jnp.dot(g_block, value_rows.T, preferred_element_type=jnp.float32)
        row_dot = jnp.sum(g_block.astype(jnp.float32) * result, axis=-1, keepdims=True)
        dscores = (weights * (dweights - row_dot)).astype(jnp.bfloat16)
        qgrad = jnp.dot(dscores, key_rows, preferred_element_type=jnp.float32) * factor
        grad_keys = (
            grad_keys + jnp.dot(dscores.T, q_block, preferred_element_type=jnp.float32) * factor
        )
        grad_values = grad_values + jnp.dot(
            weights_low.T, g_block, preferred_element_type=jnp.float32
        )
        return ((grad_keys, grad_values), (result, qgrad))

    zeros = jnp.zeros(key_rows.shape, jnp.float32)
    sliced = (
        queries.reshape(count, block, width),
        out_grads.reshape(count, block, width),
        positions.reshape(count, block),
    )
    (grad_keys, grad_values), (results, qgrads) = lax.scan(block_step, (zeros, zeros), sliced)
    return (
        results.reshape(total_rows, width),
        qgrads.reshape(total_rows, width),
        grad_keys,
        grad_values,
    )


def body(query_pre, key_pre, value_pre, grad_pre, query_ans, key_ans, value_ans, grad_ans, lengths):
    group = QH // KVH
    seq_index = lax.axis_index("seq")
    kvh_index = lax.axis_index("kvh")
    ans_index = lax.axis_index("ans")
    ans_count = lax.axis_size("ans")
    pre_rows = query_pre.shape[0]
    pre_heads = query_pre.shape[1] // DH
    kv_count = key_pre.shape[1] // DH
    ans_rows = query_ans.shape[1]
    all_keys, all_values = (
        lax.all_gather(key_pre, "seq", axis=0, tiled=True),
        lax.all_gather(value_pre, "seq", axis=0, tiled=True),
    )
    prefix = all_keys.shape[0]
    own_keys, own_values = (
        lax.all_gather(key_ans, "ans", axis=1, tiled=True),
        lax.all_gather(value_ans, "ans", axis=1, tiled=True),
    )
    first_head = (kvh_index * ans_count + ans_index) * pre_heads
    kv_slot = first_head // group - kvh_index * kv_count
    pre_positions = (
        seq_index * pre_rows + jnp.arange(pre_rows * pre_heads, dtype=jnp.int32) // pre_heads
    )
    pre_result, pre_qgrad, pre_kpart, pre_vpart = attend(
        query_pre.reshape(pre_rows * pre_heads, DH),
        all_keys,
        all_values,
        grad_pre.reshape(pre_rows * pre_heads, DH),
        pre_positions,
        0,
    )
    ans_positions = ans_index * ans_rows + jnp.arange(ans_rows * group, dtype=jnp.int32) // group
    live_rows = (ans_positions < lengths[seq_index]).astype(jnp.float32)
    query_rows = query_ans[0].reshape(ans_rows, kv_count, group * DH)
    grad_rows = grad_ans[0].reshape(ans_rows, kv_count, group * DH)
    results, qgrads, kparts, vparts = ([], [], [], [])
    key_rows = jnp.concatenate([all_keys, own_keys[0, :, 0:DH]], 0)
    value_rows = jnp.concatenate([all_values, own_values[0, :, 0:DH]], 0)
    queries = query_rows[:, 0].reshape(ans_rows * group, DH)
    masked = (grad_rows[:, 0].reshape(ans_rows * group, DH) * live_rows[:, None]).astype(
        jnp.bfloat16
    )
    result, qgrad, kpart, vpart = attend(
        queries, key_rows, value_rows, masked, ans_positions, prefix
    )
    results.append((result * live_rows[:, None]).reshape(ans_rows, group * DH))
    qgrads.append(qgrad.reshape(ans_rows, group * DH))
    kparts.append(kpart)
    vparts.append(vpart)
    answer_out = results[0][None].astype(jnp.bfloat16)
    answer_qgrad = qgrads[0][None].astype(jnp.bfloat16)
    slot_mask = (jnp.arange(kv_count, dtype=jnp.int32) == kv_slot).astype(jnp.float32)[
        None, :, None
    ]
    pre_kgrads = (
        jnp.stack([piece[:prefix] for piece in kparts], 1) + slot_mask * pre_kpart[:, None, :]
    )
    pre_vgrads = (
        jnp.stack([piece[:prefix] for piece in vparts], 1) + slot_mask * pre_vpart[:, None, :]
    )
    pre_kgrads = pre_kgrads.reshape(prefix, kv_count * DH)
    pre_vgrads = pre_vgrads.reshape(prefix, kv_count * DH)
    part_keys, part_values = (
        lax.psum_scatter(pre_kgrads, "seq", scatter_dimension=0, tiled=True),
        lax.psum_scatter(pre_vgrads, "seq", scatter_dimension=0, tiled=True),
    )
    whole_keys, whole_values = lax.psum((part_keys, part_values), "ans")
    prefix_kgrad = whole_keys.astype(jnp.bfloat16)
    prefix_vgrad = whole_values.astype(jnp.bfloat16)
    ans_kgrads = jnp.concatenate([piece[prefix:] for piece in kparts], 1)
    ans_vgrads = jnp.concatenate([piece[prefix:] for piece in vparts], 1)
    own_kgrad, own_vgrad = (
        lax.psum_scatter(ans_kgrads, "ans", scatter_dimension=0, tiled=True),
        lax.psum_scatter(ans_vgrads, "ans", scatter_dimension=0, tiled=True),
    )
    prefix_out = pre_result.reshape(pre_rows, pre_heads * DH).astype(jnp.bfloat16)
    prefix_qgrad = pre_qgrad.reshape(pre_rows, pre_heads * DH).astype(jnp.bfloat16)
    return (
        prefix_out,
        prefix_qgrad,
        prefix_kgrad,
        prefix_vgrad,
        answer_out,
        answer_qgrad,
        own_kgrad[None].astype(jnp.bfloat16),
        own_vgrad[None].astype(jnp.bfloat16),
    )


def solution(mesh):
    in_specs = (
        P("seq", ("kvh", "ans")),
        P("seq", "kvh"),
        P("seq", "kvh"),
        P("seq", ("kvh", "ans")),
        P("seq", "ans", "kvh"),
        P("seq", "ans", "kvh"),
        P("seq", "ans", "kvh"),
        P("seq", "ans", "kvh"),
        P(),
    )
    out_specs = (
        P("seq", ("kvh", "ans")),
        P("seq", ("kvh", "ans")),
        P("seq", "kvh"),
        P("seq", "kvh"),
        P("seq", "ans", "kvh"),
        P("seq", "ans", "kvh"),
        P("seq", "ans", "kvh"),
        P("seq", "ans", "kvh"),
    )
    return jax.shard_map(body, mesh=mesh, in_specs=in_specs, out_specs=out_specs, check_vma=False)
```

profile of v0, /device:TPU:22, one launch (start us, length us, event | category | flops | bytes accessed | tf_op | source)
XLA Modules:
  0.0 723.6 jit_solution(5059986928725416765)
XLA Ops:
  7.3 1.2 dynamic_slice.31
  8.5 0.7 compare_convert_fusion
  9.2 1.1 reshape.143
  10.3 55.5 %all_gather.12 = bf16[2048,128]{1,0:T(8,128)(2,1)S(1)} all-gather(bf16[128,128]{1,0:T(8,128)(2,1)} %param.12), channel_id=1, replica_groups=mesh['seq'=16,'kvh'=8,'ans'=4] {'seq'}, dimensions={0}, use_global_device_ids=true | all-gather | bytes 557056 | tf_op jit(solution)/shard_map/all_gather | solution.py:69
  65.7 13.5 %all_gather.14 = bf16[1,512,128]{2,1,0:T(8,128)(2,1)S(1)} all-gather(bf16[1,128,128]{2,1,0:T(8,128)(2,1)} %param.16), channel_id=1, replica_groups=mesh['seq'=16,'kvh'=8,'ans'=4] {'ans'}, dimensions={1}, use_global_device_ids=true | all-gather | bytes 163840 | tf_op jit(solution)/shard_map/all_gather | solution.py:74
  79.3 49.2 %all_gather.13 = bf16[2048,128]{1,0:T(8,128)(2,1)S(1)} all-gather(bf16[128,128]{1,0:T(8,128)(2,1)} %param.13), channel_id=1, replica_groups=mesh['seq'=16,'kvh'=8,'ans'=4] {'seq'}, dimensions={0}, use_global_device_ids=true | all-gather | bytes 557056 | tf_op jit(solution)/shard_map/all_gather | solution.py:70
  128.5 14.1 %all_gather.15 = bf16[1,512,128]{2,1,0:T(8,128)(2,1)} all-gather(bf16[1,128,128]{2,1,0:T(8,128)(2,1)S(1)} %copy-done.16), channel_id=1, replica_groups=mesh['seq'=16,'kvh'=8,'ans'=4] {'ans'}, dimensions={1}, use_global_device_ids=true | all-gather | bytes 163840 | tf_op jit(solution)/shard_map/all_gather | solution.py:75
  142.6 0.8 reshape_reshape_squeeze_reshape_squeeze.3
  143.4 0.9 multiply_convert_fusion.2
  144.3 0.9 pad_maximum_fusion
  145.3 45.5 %while.6 = (s32[]{:T(128)}, f32[2560,128]{1,0:T(8,128)S(1)}, f32[2560,128]{1,0:T(8,128)}, f32[2,512,128]{2,1,0:T(8,128)}, bf16[2,512,128]{2,1,0:T(8,128)(2,1)}, ...) while((s32[]{:T(128)}, f32[2560,128]{1,0:T(8,128)S(1)}, ...), condition=%wide.region_7.8_spmd.clone.clone, body=%wide.region_3.7_spmd.clone.clone.sunk | while | flops 2033520128 | bytes 107133776 | solution.py:49
  145.3 2.6 fusion.81
  147.9 0.9 fusion.82
  148.8 3.3 fusion.83
  152.1 0.9 constant_dynamic-slice_fusion.5
  153.0 0.1 copy.38
  153.2 3.6 multiply_reduce_fusion.3
  156.8 0.4 copy-done
  157.2 2.4 multiply_convert_fusion.4
  159.6 3.2 fusion.84
  162.8 0.9 fusion.85
  163.8 0.7 copy-done.13
  164.5 2.0 convolution_add_fusion.2
  166.5 0.1 copy.39
  166.6 0.7 constant_dynamic-update-slice_fusion.2
  167.4 2.7 fusion.81
  170.0 0.9 fusion.82
  170.9 3.3 fusion.83
  174.2 0.9 constant_dynamic-slice_fusion.5
  175.1 0.1 copy.38
  175.2 3.6 multiply_reduce_fusion.3
  178.9 0.4 copy-done
  179.3 2.4 multiply_convert_fusion.4
  181.6 3.2 fusion.84
  184.9 0.9 fusion.85
  185.8 0.7 copy-done.13
  186.5 3.3 convolution_add_fusion.2
  189.9 0.1 copy.39
  190.0 0.7 constant_dynamic-update-slice_fusion.2
  190.7 1.7 slice.15
  192.5 0.7 slice.14
  193.3 0.9 squeeze.36
  194.2 1.7 fusion.39
  195.8 1.4 copy-done.4
  197.2 0.4 fusion.24
  197.7 3.6 fusion.21
  201.3 0.2 reduce-scatter.5.cloned.1.call-start
  201.7 2.4 multiply_reduce_fusion.1
  204.1 0.6 fusion.20
  204.7 1.5 fusion.22
  206.3 0.4 fusion.25
  206.7 0.7 convert_element_type.116
  207.5 0.7 convert_element_type.112
  208.2 0.7 fusion.33
  209.0 0.2 mul.122
  209.3 0.8 convert_element_type.127
  210.1 0.8 multiply_convert_fusion.1
  210.9 10.1 %reduce-scatter.11.cloned.1.call-done = f32[128,128]{1,0:T(8,128)} async-done(((f32[512,128]{1,0:T(8,128)}), f32[128,128]{1,0:T(8,128)}) %reduce-scatter.11.cloned.1.call-update) | async-done | bytes 65552 | tf_op jit(solution)/shard_map/reduce_scatter | solution.py:132
  221.0 1.5 convert_bitcast_fusion
  222.4 28.0 %reduce-scatter.9.cloned.1.call-done = f32[128,128]{1,0:T(8,128)} async-done(((f32[512,128]{1,0:T(8,128)}), f32[128,128]{1,0:T(8,128)}) %reduce-scatter.9.cloned.1.call-update) | async-done | bytes 65552 | tf_op jit(solution)/shard_map/reduce_scatter | solution.py:131
  250.4 1.5 convert_bitcast_fusion.1
  251.9 223.3 %reduce-scatter.7.cloned.1.call-done = f32[128,128]{1,0:T(8,128)} async-done(((f32[2048,128]{1,0:T(8,128)}), f32[128,128]{1,0:T(8,128)}) %reduce-scatter.7.cloned.1.call-update) | async-done | bytes 65552 | tf_op jit(solution)/shard_map/reduce_scatter | solution.py:123
  475.2 221.8 %reduce-scatter.5.cloned.1.call-done = f32[128,128]{1,0:T(8,128)} async-done(((f32[2048,128]{1,0:T(8,128)}), f32[128,128]{1,0:T(8,128)}) %reduce-scatter.5.cloned.1.call-update) | async-done | bytes 65552 | tf_op jit(solution)/shard_map/reduce_scatter | solution.py:122
  697.0 20.1 %all-reduce.2 = (bf16[128,128]{1,0:T(8,128)(2,1)}, bf16[128,128]{1,0:T(8,128)(2,1)}) all-reduce(f32[128,128]{1,0:T(8,128)} %reduce-scatter.5.cloned.1.call-done, f32[128,128]{1,0:T(8,128)} %reduce-scatter.7.cloned.1.call-done), channel_id=1, replica_groups=mesh['seq'=16,'kvh'=8,'ans'=4] {'ans'}, use_global_device_ids=true, to_apply=%region_9.10 | all-reduce | flops 32768 | bytes 196608 | tf_op jit(solution)/shard_map/psum | solution.py:125
  (75 shorter events, 0.9 us)
Async XLA Ops:
  7.2 121.3 %copy-start.16 = (bf16[1,128,128]{2,1,0:T(8,128)(2,1)S(1)}, bf16[1,128,128]{2,1,0:T(8,128)(2,1)}, u32[]{:S(2)}) copy-start(bf16[1,128,128]{2,1,0:T(8,128)(2,1)} %param.17) | copy-start | bytes 98308
  7.2 135.4 %copy-start.11 = (bf16[1,128,1024]{2,1,0:T(8,128)(2,1)S(1)}, bf16[1,128,1024]{2,1,0:T(8,128)(2,1)}, u32[]{:S(2)}) copy-start(bf16[1,128,1024]{2,1,0:T(8,128)(2,1)} %param.15) | copy-start | bytes 786436
  7.2 213.8 %reduce-scatter.11.cloned.1.call-start = ((), (), s32[]{:S(2)}) async-start(), calls=%async_computation.7 | async-start | bytes 327680 | tf_op jit(solution)/shard_map/reduce_scatter | solution.py:132
  65.7 79.5 %copy-start.2 = (bf16[2048,128]{1,0:T(8,128)(2,1)}, bf16[2048,128]{1,0:T(8,128)(2,1)S(1)}, u32[]{:S(2)}) copy-start(bf16[2048,128]{1,0:T(8,128)(2,1)S(1)} %all_gather.12) | copy-start | bytes 1572868
  128.5 16.7 %copy-start.6 = (bf16[2048,128]{1,0:T(8,128)(2,1)}, bf16[2048,128]{1,0:T(8,128)(2,1)S(1)}, u32[]{:S(2)}) copy-start(bf16[2048,128]{1,0:T(8,128)(2,1)S(1)} %all_gather.13) | copy-start | bytes 1572868
  143.4 1.8 copy-start.9
  153.1 4.0 copy-start
  157.2 7.3 %slice-start = ((s8[5242880]{0:T(1024)(128)(4,1)}), s8[1048576]{0:T(1024)(128)(4,1)S(1)}, s32[]{:S(2)}) async-start(s8[5242880]{0:T(1024)(128)(4,1)} %bitcast.72), calls=%async_computation.8 | async-start | bytes 2097152 | tf_op jit(solution)/shard_map/while
  159.6 3.3 copy-start.1
  159.6 3.3 copy-start.8
  159.6 3.3 copy-start.12
  159.6 4.9 slice-start.1
  163.7 0.7 copy-start.13
  175.2 4.0 copy-start
  179.3 7.3 %slice-start = ((s8[5242880]{0:T(1024)(128)(4,1)}), s8[1048576]{0:T(1024)(128)(4,1)S(1)}, s32[]{:S(2)}) async-start(s8[5242880]{0:T(1024)(128)(4,1)} %bitcast.72), calls=%async_computation.8 | async-start | bytes 2097152 | tf_op jit(solution)/shard_map/while
  181.6 3.3 copy-start.1
  181.6 3.3 copy-start.8
  181.6 3.3 copy-start.12
  181.6 4.9 slice-start.1
  185.8 0.7 copy-start.13
  192.4 58.0 %reduce-scatter.9.cloned.1.call-start = ((), (), s32[]{:S(2)}) async-start(), calls=%async_computation.6 | async-start | bytes 327680 | tf_op jit(solution)/shard_map/reduce_scatter | solution.py:131
  193.2 281.9 %reduce-scatter.7.cloned.1.call-start = ((), (), s32[]{:S(2)}) async-start(), calls=%async_computation.5 | async-start | bytes 1114112 | tf_op jit(solution)/shard_map/reduce_scatter | solution.py:123
  194.2 3.5 copy-start.15
  195.8 1.4 copy-start.4
  197.7 4.0 copy-start.7
  201.3 495.7 %reduce-scatter.5.cloned.1.call-start = ((), (), s32[]{:S(2)}) async-start(), calls=%async_computation.4 | async-start | bytes 1114112 | tf_op jit(solution)/shard_map/reduce_scatter | solution.py:122
  201.7 2.4 copy-start.5
  204.7 1.5 copy-start.3
  206.2 1.9 copy-start.10
  206.2 3.0 copy-start.14
Sparse Core Ops, SparseCore 0:
  192.5 28.3 reduce-scatter.10
  224.0 26.3 reduce-scatter.8
  254.9 220.2 reduce-scatter.6
  480.1 216.7 reduce-scatter.4
where the time goes:
time: 724 us
  waiting for transfers between devices  483 us (67%)
  blocking collectives  152 us (21%)
  matrix products  41.1 us (6%)
  local copies, waits for them, and re-layouts  16.6 us (2%)
  other arithmetic  15.6 us (2%)
  between operations  14.1 us (2%)
    reduce_scatter x1, waiting for transfers between devices, body(): lax.psum_scatter(pre_vgrads, 'seq', scatter_dimension=0, tiled=True)  223 us
    reduce_scatter x1, waiting for transfers between devices, body(): lax.psum_scatter(pre_kgrads, 'seq', scatter_dimension=0, tiled=True)  222 us
    all_gather x1, blocking collectives, body(): lax.all_gather(key_pre, 'seq', axis=0, tiled=True)  55.5 us
    all_gather x1, blocking collectives, body(): lax.all_gather(value_pre, 'seq', axis=0, tiled=True)  49.2 us
    reduce_scatter x1, waiting for transfers between devices, body(): lax.psum_scatter(ans_kgrads, 'ans', scatter_dimension=0, tiled=True)  28 us
    psum x1, blocking collectives, body(): whole_keys, whole_values = lax.psum((part_keys, part_values), 'ans')  20.1 us
  transfers between devices with their start and end apart: 4, of which 4 were waited for; matrix products, arithmetic and copies ran while one was open for 3% of the time, Pallas kernels for 0%

commit v1 on v0

v1 whole, which is shorter than its diff:
```python
import functools
import math

import jax
import jax.numpy as jnp
from jax import lax
from jax.experimental import pallas as pl
from jax.experimental.pallas import tpu as pltpu
from jax.sharding import PartitionSpec as P

MESH = pl.DeviceIdType.MESH
F32, BF16 = jnp.float32, jnp.bfloat16
DH = 128
FACTOR = 1.0 / math.sqrt(DH)
SCALE = FACTOR * math.log2(math.e)
HIDDEN = -1e30
RA, RP = 1024, 256
R = RA + RP


def nn(a, b):
    return lax.dot_general(a, b, (((1,), (0,)), ((), ())), preferred_element_type=F32)


def tn(a, b):
    return lax.dot_general(a, b, (((0,), (0,)), ((), ())), preferred_element_type=F32)


def turn(x):
    return x.astype(F32).T


def kernel(
    qp, kp, vp, gp, qa, ka, va, ga, lengths,
    po, pq, pk, pv, ao, aq, ak, av,
    qin, gin, q_t, q_r, g_t, gs_t, gs_r, k_all, v_all, own, s_all, s_own, top, total, e_all, e_own, ds_all, ds_own,
    o_t, rowdot, gk_s, gk_r, gv_s, gv_r, acc_k, acc_v, part_k, part_v, got_k, got_v, fin, ga_own, ga_s,
    ga_r,
    in_sem, kz_ss, kz_rs, k_ss, k_rs, va_ss, va_rs, v_ss, v_rs, own_ss, own_rs, gk_ss, gk_rs, gv_ss, gv_rs,
    two_ss, two_rs, fin_ss, fin_rs, ga_ss, ga_rs,
):
    seq, q = lax.axis_index("seq"), lax.axis_index("ans")
    zh, y = lax.div(seq, 8), lax.rem(seq, 8)
    z = zh * 4 + q
    wrap = lambda i: lax.rem(i + 8, 8)
    at_y = lambda i: {"seq": zh * 8 + i, "ans": q}
    at_z = lambda i: {"seq": lax.div(i, 4) * 8 + y, "ans": lax.rem(i, 4)}
    peers = (lambda i: at_y(wrap(y + i)), lambda i: at_z(wrap(z + i)))

    def remote(src, dst, send, recv, dev):
        return pltpu.make_async_remote_copy(
            src_ref=src, dst_ref=dst, send_sem=send, recv_sem=recv, device_id=dev, device_id_type=MESH
        )

    loads = [
        pltpu.make_async_copy(qa.at[0], qin.at[:, pl.ds(0, RA)], in_sem.at[0]),
        pltpu.make_async_copy(qp, qin.at[:, pl.ds(RA, RP)], in_sem.at[1]),
        pltpu.make_async_copy(ga.at[0], gin.at[:, pl.ds(0, RA)], in_sem.at[2]),
        pltpu.make_async_copy(gp, gin.at[:, pl.ds(RA, RP)], in_sem.at[3]),
        pltpu.make_async_copy(kp, k_all.at[zh, y], in_sem.at[4]),
        pltpu.make_async_copy(vp.at[pl.ds(q * 32, 32)], v_all.at[zh, y, q], in_sem.at[5]),
        pltpu.make_async_copy(ka.at[0], own.at[q, 0], in_sem.at[6]),
        pltpu.make_async_copy(va.at[0], own.at[q, 1], in_sem.at[7]),
    ]
    for copy in loads:
        copy.start()

    barrier = pltpu.get_barrier_semaphore()
    for i in range(1, 8):
        for peer in peers:
            pl.semaphore_signal(barrier, inc=1, device_id=peer(i), device_id_type=MESH)
    pl.semaphore_wait(barrier, 14)

    half = (zh, 1 - zh)
    far = lax.rem(seq + 8, 16)
    steps = (1, -1, 2, -2)

    def key_copy(h, stage, n, came=False):
        sign, hop = (1 - 2 * (n % 2)), steps[n]
        back = (0 if stage == 1 else 2 * sign) + (hop if came else 0)
        at = k_all.at[half[h], wrap(y - back)]
        if stage == 2 and n >= 2:
            at = k_all.at[half[h], wrap(y - back), pl.ds(64 * (n % 2), 64)]
        src = kp if (stage == 1 and h == 0 and not came) else at
        return remote(src, at, k_ss.at[h, stage - 1, n], k_rs.at[h, stage - 1, n], peers[0](hop))

    def cross(i, to):
        return remote(kp, k_all.at[zh, y], kz_ss.at[i], kz_rs.at[0], {"seq": far, "ans": to})

    crossing = [(0, (3, 2)), (3, (0, 1))]
    for who, targets in crossing:
        @pl.when(q == who)
        def _():
            for i, to in enumerate(targets):
                cross(i, to).start()

    def quarter(i):
        return remote(
            vp.at[pl.ds(q * 32, 32)], v_all.at[zh, y, q], va_ss.at[i], va_rs.at[i], peers[0](i)
        )

    for i in (4, 3, -3, 2, -2, 1, -1):
        quarter(i % 8).start()
    for n in (2, 3, 0, 1):
        key_copy(0, 1, n).start()

    def value_copy(stage, n, came=False):
        sign, hop = (1 - 2 * (n % 2)), steps[n]
        at = wrap(z - ((0 if stage == 1 else 2 * sign) + (hop if came else 0)))
        block = v_all.at[lax.div(at, 4), :, lax.rem(at, 4)]
        if stage == 2 and n >= 2:
            block = v_all.at[lax.div(at, 4), pl.ds(4 * (n % 2), 4), lax.rem(at, 4)]
        return remote(block, block, v_ss.at[stage - 1, n], v_rs.at[stage - 1, n], peers[1](hop))

    def own_copy(j, side, to):
        return remote(
            (ka, va)[side].at[0], own.at[j, side], own_ss.at[to, side], own_rs.at[j, side], {"seq": seq, "ans": to}
        )

    for to in range(1, 4):
        @pl.when(q < to)
        def _():
            for side in range(2):
                own_copy(q, side, to).start()

    def drain_gather():
        for stage in range(1, 3):
            for n in range(4):
                for h in range(2):
                    key_copy(h, stage, n).wait_send()
                value_copy(stage, n).wait_send()
        for who, targets in crossing:
            @pl.when(q == who)
            def _():
                for i, to in enumerate(targets):
                    cross(i, to).wait_send()
        for i in range(1, 8):
            quarter(i).wait_send()
        for to in range(1, 4):
            @pl.when(q < to)
            def _():
                for side in range(2):
                    own_copy(q, side, to).wait_send()

    for copy in loads:
        copy.wait()
    lane = lax.rem(lax.broadcasted_iota(jnp.int32, (1, R), 1), 128)
    live = ((q * 128 + lane) < lengths[seq]) | (lax.broadcasted_iota(jnp.int32, (1, R), 1) >= RA)
    live = jnp.where(live, 1.0, 0.0)
    for h in range(R // 128):
        cols = slice(h * 128, h * 128 + 128)
        q_r[cols, :] = qin[:, cols]
        q_t[:, cols] = turn(qin[:, cols]).astype(BF16)
        g_t[:, cols] = (turn(gin[:, cols]) * live[:, cols]).astype(BF16)
    top[...] = jnp.full(top.shape, HIDDEN, F32)

    remote(kp, k_all.at[half[1], y], kz_ss.at[0], kz_rs.at[0], {"seq": far, "ans": q}).wait_recv()
    for n in (2, 3, 0, 1):
        key_copy(1, 1, n).start()

    def scores(j):
        keys = k_all[:, j].reshape(256, DH)
        s = nn(keys, q_t[:, :RA])
        s_all[:, j, :, :RA] = s.reshape(2, 128, RA)
        top[:, :RA] = jnp.maximum(top[:, :RA], s.reshape(32, 8, RA).max(0))
        s = nn(keys, q_t[:, RA:]).reshape(2, 128, RP)
        at_key = (
            lax.broadcasted_iota(jnp.int32, (2, 128, RP), 0) * 1024
            + j * 128
            + lax.broadcasted_iota(jnp.int32, (2, 128, RP), 1)
        )
        at_row = seq * 128 + lax.rem(lax.broadcasted_iota(jnp.int32, (2, 128, RP), 2), 128)
        s = jnp.where(at_key <= at_row, s, HIDDEN)
        s_all[:, j, :, RA:] = s
        top[:, RA:] = jnp.maximum(top[:, RA:], s.reshape(32, 8, RP).max(0))

    def hand_on(h):
        for n in (2, 3):
            key_copy(h, 1, n, came=True).wait_recv()
            key_copy(h, 2, n - 2).start()
            key_copy(h, 2, n).start()

    hand_on(0)
    for i in range(1, 8):
        src = wrap(y - i)
        remote(
            v_all.at[zh, src, q], v_all.at[zh, src, q], va_ss.at[i], va_rs.at[i], peers[0](i)
        ).wait_recv()
    for n in (2, 3, 0, 1):
        value_copy(1, n).start()
    scores(y)
    hand_on(1)
    for n in range(2):
        for h in range(2):
            key_copy(h, 1, n, came=True).wait_recv()
    for n in range(4):
        scores(wrap(y - steps[n]))
    for n in (2, 3):
        value_copy(1, n, came=True).wait_recv()
        value_copy(2, n - 2).start()
        value_copy(2, n).start()
    for n in range(4):
        for h in range(2):
            key_copy(h, 2, n, came=True).wait_recv()
    for n in (3, -3, 4):
        scores(wrap(y + n))

    def own_scores(j, _):
        s = nn(own[j, 0], q_t[:, :RA])
        key = lax.broadcasted_iota(jnp.int32, (128, RA), 0) + j * 128
        row = lax.rem(lax.broadcasted_iota(jnp.int32, (128, RA), 1), 128) + q * 128
        s = jnp.where(key <= row, s, HIDDEN)
        s_own[j] = s
        top[:, :RA] = jnp.maximum(top[:, :RA], s.reshape(16, 8, RA).max(0))
        return 0

    for j in range(3):
        @pl.when(q > j)
        def _():
            for side in range(2):
                own_copy(j, side, q).wait_recv()
    lax.fori_loop(0, q + 1, own_scores, 0)

    best = top[...].max(0, keepdims=True)
    top[0:1, :] = best
    total[...] = jnp.zeros_like(total)
    o_t[...] = jnp.zeros_like(o_t)

    def own_exp(j, _):
        e = jnp.exp2((s_own[j] - top[0:1, :RA]) * SCALE)
        total[:, :RA] += e.reshape(16, 8, RA).sum(0)
        e = e.astype(BF16)
        e_own[j] = e
        o_t[:, :RA] += tn(own[j, 1], e)
        return 0

    lax.fori_loop(0, q + 1, own_exp, 0)

    def exps(j, _):
        e = jnp.exp2((s_all[:, j].reshape(256, R) - top[0:1, :]) * SCALE)
        total[...] += e.reshape(32, 8, R).sum(0)
        e_all[:, j] = e.astype(BF16).reshape(2, 4, 32, R)
        return 0

    lax.fori_loop(0, 8, exps, 0)
    inverse = 1.0 / total[...].sum(0, keepdims=True)
    for h in range(R // 128):
        cols = slice(h * 128, h * 128 + 128)
        g = (g_t[:, cols].astype(F32) * inverse[:, cols]).astype(BF16)
        gs_t[:, cols] = g
        gs_r[cols, :] = turn(g).astype(BF16)

    def value_pair(j):
        return nn(e_all[:, j].reshape(256, R), gs_r[...]).reshape(2, 128, DH)

    def key_part(at):
        hi, lo = lax.div(at, 4), lax.rem(at, 4)
        dp = nn(v_all[hi, :, lo].reshape(256, DH), gs_t[...])
        e = e_all[hi, :, lo].reshape(256, R).astype(F32)
        ds = (e * (dp - rowdot[...])).astype(BF16)
        ds_all[hi, :, lo] = ds.reshape(8, 32, R)
        return nn(ds, q_r[...]).reshape(2, 128, DH)

    values = (0, y, value_pair, gv_s, gv_r, gv_ss, gv_rs, 1, z, acc_v, part_v, got_v, 1)
    keys = (1, z, key_part, gk_s, gk_r, gk_ss, gk_rs, 0, y, acc_k, part_k, got_k, 0)

    hops = {4: 2, 3: 1, 2: 2, 1: 1}

    def grad_copy(ring, d, k):
        axis, _, _, out, came, ss, rs = ring[:7]
        src, dst = out.at[d, k - 1], came.at[d, k - 1]
        if k == 4:
            src, dst = src.at[d], dst.at[d]
        return remote(src, dst, ss.at[d, k - 1], rs.at[d, k - 1], peers[axis]((1 - 2 * d) * hops[k]))

    def send_first(ring):
        axis, me, part, out = ring[:4]
        piece = part(wrap(me + 4)).astype(BF16)
        for d in range(2):
            out[d, 3, d] = piece[d]
            grad_copy(ring, d, 4).start()
        send_plain(ring, 3)

    def send_plain(ring, k):
        axis, me, part, out = ring[:4]
        for d in range(2):
            out[d, k - 1] = part(wrap(me + (1 - 2 * d) * k)).astype(BF16)
            grad_copy(ring, d, k).start()

    def send_second(ring):
        axis, me, part, out, came = ring[:5]
        pieces = [part(wrap(me + (1 - 2 * d) * 2)) for d in range(2)]
        for d in range(2):
            grad_copy(ring, d, 3).wait_recv()
            grad_copy(ring, d, 4).wait_recv()
            piece = pieces[d] + came[d, 2].astype(F32)
            out[d, 1, d] = (piece[d] + came[d, 3, d].astype(F32)).astype(BF16)
            out[d, 1, 1 - d] = piece[1 - d].astype(BF16)
            grad_copy(ring, d, 2).start()

    def add_own(ring):
        acc = ring[9]
        acc[...] = ring[2](ring[1]).reshape(acc.shape)

    def two_copy(ring, i):
        axis, me, _, sent, got, n = ring[7:]
        return remote(sent.at[wrap(me + i)], got.at[me], two_ss.at[n, i], two_rs.at[n, i], peers[axis](i))

    def exchange(ring):
        came, acc, sent = ring[4], ring[9], ring[10]
        whole = acc[...]
        for d in range(2):
            for k in range(2):
                grad_copy(ring, d, k + 1).wait_recv()
                whole = whole + came[d, k].astype(F32).reshape(acc.shape)
        acc[...] = whole
        sent[...] = whole.astype(BF16)
        for i in (4, 3, -3, 2, -2, 1, -1):
            two_copy(ring, i % 8).start()

    def fin_copy(n, i):
        other = lax.rem(q + i, 4)
        return remote(fin.at[n, q], fin.at[n, q], fin_ss.at[n, i], fin_rs.at[n, i], {"seq": seq, "ans": other})

    def finish(ring):
        axis, me, acc, sent, got, n = ring[7:]
        piece = acc[me]
        for i in range(1, 8):
            src = wrap(me - i)
            remote(
                sent.at[src], got.at[src], two_ss.at[n, i], two_rs.at[n, i], peers[axis](i)
            ).wait_recv()
            piece = piece + got[src].astype(F32)
        fin[n, q] = (piece * (FACTOR if n == 0 else 1.0)).astype(BF16)
        for i in range(1, 4):
            fin_copy(n, i).start()

    send_first(values)

    for n in range(2):
        value_copy(1, n, came=True).wait_recv()
    for n in range(4):
        value_copy(2, n, came=True).wait_recv()

    for c in range(R // 256):
        cols = slice(c * 256, c * 256 + 256)
        o = o_t[:, cols] + tn(v_all[...].reshape(2048, DH), e_all[:, :, :, :, cols].reshape(2048, 256))
        o = o * inverse[:, cols]
        rowdot[:, cols] = (gs_t[:, cols].astype(F32) * o).sum(0, keepdims=True)
        o_t[:, cols] = o * live[:, cols]

    send_first(keys)
    send_plain(values, 1)
    send_plain(keys, 1)
    send_second(values)
    add_own(values)
    add_own(keys)
    send_second(keys)

    def ans_copy(j, src):
        return remote(
            ga_s.at[j], ga_r.at[src], ga_ss.at[j], ga_rs.at[src], {"seq": seq, "ans": j}
        )

    def own_grads(j):
        e = e_own[j]
        dv = nn(e, gs_r[:RA, :])
        dp = nn(own[j, 1], gs_t[:, :RA])
        ds = (e.astype(F32) * (dp - rowdot[:, :RA])).astype(BF16)
        ds_own[j] = ds
        return nn(ds, q_r[:RA, :]), dv

    def send_own(j, _):
        dk, dv = own_grads(j)
        ga_s[j, 0] = dk.astype(BF16)
        ga_s[j, 1] = dv.astype(BF16)
        ans_copy(j, q).start()
        return 0

    lax.fori_loop(0, q, send_own, 0)
    exchange(values)
    dk, dv = own_grads(q)
    ga_own[0], ga_own[1] = dk, dv

    def rows_out(of_answers, of_prompt):
        for h in range(R // 128):
            tile = o_t[:, h * 128 : h * 128 + 128].T.astype(BF16)
            if h < RA // 128:
                of_answers[0, :, h * 128 : h * 128 + 128] = tile
            else:
                of_prompt[:, h * 128 - RA : h * 128 - RA + 128] = tile

    rows_out(ao, po)
    exchange(keys)
    finish(values)

    o_t[...] = tn(k_all[...].reshape(2048, DH), ds_all[...].reshape(2048, R))

    def own_query(j, _):
        o_t[:, :RA] += tn(own[j, 0], ds_own[j])
        return 0

    lax.fori_loop(0, q + 1, own_query, 0)
    o_t[...] = o_t[...] * FACTOR
    finish(keys)
    rows_out(aq, pq)

    for src in range(1, 4):
        @pl.when(q < src)
        def _():
            remote(
                ga_s.at[0], ga_r.at[src], ga_ss.at[0], ga_rs.at[src], {"seq": seq, "ans": q}
            ).wait_recv()
            ga_own[...] += ga_r[src].astype(F32)

    ak[0] = (ga_own[0] * FACTOR).astype(BF16)
    av[0] = ga_own[1].astype(BF16)

    drain_gather()
    for ring in (values, keys):
        for d in range(2):
            for k in range(1, 5):
                grad_copy(ring, d, k).wait_send()
        for i in range(1, 8):
            two_copy(ring, i).wait_send()
    for j in range(3):
        @pl.when(j < q)
        def _():
            ans_copy(j, q).wait_send()
    for n, out in ((1, pv), (0, pk)):
        for i in range(1, 4):
            src = lax.rem(q - i + 4, 4)
            remote(
                fin.at[n, src], fin.at[n, src], fin_ss.at[n, i], fin_rs.at[n, i], {"seq": seq, "ans": src}
            ).wait_recv()
        out[...] = fin[n].reshape(128, DH)
        for i in range(1, 4):
            fin_copy(n, i).wait_send()


def hand_out(*refs):
    sem = refs[16]
    copies = [pltpu.make_async_copy(refs[i], refs[8 + i], sem.at[i]) for i in range(8)]
    for copy in copies:
        copy.start()
    for copy in copies:
        copy.wait()


def body(query_pre, key_pre, value_pre, grad_pre, query_ans, key_ans, value_ans, grad_ans, lengths):
    shapes = [query_pre, query_pre, key_pre, value_pre, query_ans, query_ans, key_ans, value_ans]
    any_spec = pl.BlockSpec(memory_space=pl.ANY)
    vm = pltpu.VMEM
    dma = pltpu.SemaphoreType.DMA
    outs = pl.pallas_call(
        kernel,
        out_shape=[vm(x.shape, BF16) for x in shapes],
        in_specs=[any_spec] * 8 + [pl.BlockSpec(memory_space=pltpu.SMEM)],
        out_specs=[pl.BlockSpec(memory_space=vm)] * 8,
        scratch_shapes=[
            vm((128, R), BF16), vm((128, R), BF16),
            vm((DH, R), BF16), vm((R, DH), BF16),
            vm((DH, R), BF16), vm((DH, R), BF16), vm((R, DH), BF16),
            vm((2, 8, 128, DH), BF16), vm((2, 8, 4, 32, DH), BF16), vm((4, 2, 128, DH), BF16),
            vm((2, 8, 128, R), F32), vm((4, 128, RA), F32), vm((8, R), F32), vm((8, R), F32),
            vm((2, 8, 4, 32, R), BF16), vm((4, 128, RA), BF16),
            vm((2, 8, 4, 32, R), BF16), vm((4, 128, RA), BF16),
            vm((DH, R), F32), vm((1, R), F32),
            vm((2, 4, 2, 128, DH), BF16), vm((2, 4, 2, 128, DH), BF16),
            vm((2, 4, 2, 128, DH), BF16), vm((2, 4, 2, 128, DH), BF16),
            vm((8, 32, DH), F32), vm((8, 32, DH), F32),
            vm((8, 32, DH), BF16), vm((8, 32, DH), BF16), vm((8, 32, DH), BF16), vm((8, 32, DH), BF16),
            vm((2, 4, 32, DH), BF16), vm((2, 128, DH), F32),
            vm((4, 2, 128, DH), BF16), vm((4, 2, 128, DH), BF16),
            dma((8,)), dma((2,)), dma((1,)), dma((2, 2, 4)), dma((2, 2, 4)), dma((8,)), dma((8,)),
            dma((2, 4)), dma((2, 4)), dma((4, 2)), dma((4, 2)), dma((2, 4)), dma((2, 4)), dma((2, 4)), dma((2, 4)),
            dma((2, 8)), dma((2, 8)), dma((2, 4)), dma((2, 4)), dma((4,)), dma((4,)),
        ],
        compiler_params=pltpu.CompilerParams(
            collective_id=0, has_side_effects=True, vmem_limit_bytes=56 * 1024 * 1024
        ),
        cost_estimate=pl.CostEstimate(flops=5_000_000_000, bytes_accessed=3_000_000, transcendentals=3_200_000),
        name="attention",
    )(query_pre, key_pre, value_pre, grad_pre, query_ans, key_ans, value_ans, grad_ans, lengths)
    return pl.pallas_call(
        hand_out,
        out_shape=[jax.ShapeDtypeStruct(x.shape, BF16) for x in shapes],
        in_specs=[any_spec] * 8,
        out_specs=[any_spec] * 8,
        scratch_shapes=[dma((8,))],
        cost_estimate=pl.CostEstimate(flops=0, bytes_accessed=1_700_000, transcendentals=0),
        name="hand_out",
    )(*[pltpu.with_memory_space_constraint(x, vm) for x in outs])


def solution(mesh):
    rows, keys = P("seq", ("kvh", "ans")), P("seq", "kvh")
    answers = P("seq", "ans", "kvh")
    return jax.shard_map(
        body,
        mesh=mesh,
        in_specs=(rows, keys, keys, rows, answers, answers, answers, answers, P()),
        out_specs=(rows, rows, keys, keys, answers, answers, answers, answers),
        check_vma=False,
    )
```

time: 724 us -> 58 us (0.08)
  the two profiles are of different devices: /device:TPU:22 before, /device:TPU:2 now
where the time goes in v1:
time: 58 us; the launch traced here: 57.9 us
  Pallas kernels  57.2 us (99%)
  between operations  0.64 us (1%)
    pallas_call x1, Pallas kernels, body(): pl.pallas_call(kernel, out_shape=[vm(x.shape, BF16) for x in shapes], in_...  56.3 us

profile of v1, /device:TPU:2, one launch (start us, length us, event | category | flops | bytes accessed | tf_op | source)
XLA Modules:
  0.0 57.9 jit_solution(6055638175763415243)
XLA Ops:
  0.6 56.3 %attention.1 = (bf16[128,256]{1,0:T(8,128)(2,1)S(1)}, bf16[128,256]{1,0:T(8,128)(2,1)S(1)}, bf16[128,128]{1,0:T(8,128)(2,1)S(1)}, bf16[128,128]{1,0:T(8,128)(2,1...) custom-call(bf16[128,256]{1,0:T(8,128)(2,1)} %qp.1, ...), custom_call_target="tpu_custom_call" | custom-call | flops 5000000000 | bytes 3000000 | tf_op jit(solution)/shard_map/attention/pallas_call | solution.py:455
  56.9 0.9 %hand_out.1 = (bf16[128,256]{1,0:T(8,128)(2,1)}, bf16[128,256]{1,0:T(8,128)(2,1)}, bf16[128,128]{1,0:T(8,128)(2,1)}, bf16[128,128]{1,0:T(8,128)(2,1)}, bf16[1,12...) custom-call(bf16[128,256]{1,0:T(8,128)(2,1)S(1)} %get-tuple-element., ...), custom_call_target="tpu_custom_call" | custom-call | bytes 1700000 | tf_op jit(solution)/shard_map/hand_out/pallas_call | solution.py:485
